TPU v7x, 256 devices: a whole 4x4x8 slice. The times are simulated.
256 devices in a mesh: chan: 32 (over z, x), slab: 2 (over core), batch: 4 (over y).
Axes of the slice: x: 4, y: 4, z: 8, core: 2. Of those that a mesh axis runs over, the one named last changes fastest.
Arguments:
- inputs: bfloat16 [2048, 8, 512], P(('batch', 'chan'), 'slab'), parts along dimension 0, may hold values from -6 to 6
- weights: bfloat16 [27, 512, 512], P(None, 'chan'), may hold values from -0.09375 to 0.09375
- out_grad: bfloat16 [2048, 8, 512], P(('batch', 'chan'), 'slab'), parts along dimension 0, may hold values from -6 to 6
Outputs:
- conv_out: bfloat16 [2048, 8, 512], P(('batch', 'chan'), 'slab'), parts along dimension 0
- input_grad: bfloat16 [2048, 8, 512], P(('batch', 'chan'), 'slab'), parts along dimension 0
There are 4 independent parts, one for each index of `batch`. A program takes and returns all parts, laid end to end along the dimension named above; an argument that names none is the same for every part. Nothing has to cross between parts.
All inputs are finite; a program needn't handle non-finite values.
Results may differ from a plain program's by a relative error of at most 0.0013.
Values may be sent and summed in bfloat16 or wider, within the bound.
A program may use at most 192 MiB of HBM per device.

v0:
```python
import jax
import jax.numpy as jnp
from jax import lax
from jax.sharding import PartitionSpec as P

NZ = 64
OFFSETS = (-1, 0, 1)


def padded(block, sides, width):
    for axis, dim in sides:
        count = lax.axis_size(axis)
        forward = [(i, i + 1) for i in range(count - 1)]
        forward.append((count - 1, 0))
        backward = [(target, source) for source, target in forward]
        low = lax.ppermute(
            lax.slice_in_dim(block, block.shape[dim] - width, None, axis=dim), axis, forward
        )
        high = lax.ppermute(lax.slice_in_dim(block, 0, width, axis=dim), axis, backward)
        block = jnp.concatenate([low, block, high], axis=dim)
    return block


def stack_yz(block, rows_y):
    chans, slab_len, plane_size = block.shape
    shaped = block.reshape(chans, slab_len, rows_y, NZ)
    pieces = []
    for offset_y in OFFSETS:
        for offset_z in OFFSETS:
            pieces.append(jnp.roll(shaped, (-offset_y, -offset_z), axis=(2, 3)))
    return jnp.stack(pieces).reshape(9 * chans, slab_len * plane_size)


def per_device(inputs, weights, out_grad):
    chans_in, slab_len, plane_size = inputs.shape
    chans_out = out_grad.shape[0]
    full_out = weights.shape[2]
    rows_y = plane_size // NZ
    cell_count = slab_len * plane_size
    halo_in = padded(inputs, (("slab", 1),), 1)
    grad_all = lax.all_gather(out_grad, "chan", axis=0, tiled=True)
    halo_grad = padded(grad_all, (("slab", 1),), 1)
    columns = [
        stack_yz(halo_in[:, 1 + offset_x : 1 + offset_x + slab_len], rows_y) for offset_x in OFFSETS
    ]
    running = jnp.zeros((chans_out * lax.axis_size("chan"), cell_count), jnp.float32)
    for partial_index_x in range(3):
        partial_weight_x = weights[9 * partial_index_x : 9 * partial_index_x + 9]
        partial_weight_x = partial_weight_x.reshape(9 * chans_in, chans_out * lax.axis_size("chan"))
        running = running + lax.dot_general(
            partial_weight_x,
            columns[partial_index_x],
            (((0,), (0,)), ((), ())),
            preferred_element_type=jnp.float32,
        )
    own_rows = lax.psum_scatter(running, "chan", scatter_dimension=0, tiled=True)
    conv_out = own_rows.astype(jnp.bfloat16).reshape(chans_out, slab_len, plane_size)
    running_grad = jnp.zeros((chans_in, slab_len, rows_y, NZ), jnp.float32)
    for index_x, offset_x in enumerate(OFFSETS):
        plane_x = halo_grad[:, 1 - offset_x : 1 - offset_x + slab_len].reshape(full_out, cell_count)
        weight_x = weights[9 * index_x : 9 * index_x + 9].reshape(9 * chans_in, full_out)
        product = lax.dot_general(
            weight_x, plane_x, (((1,), (0,)), ((), ())), preferred_element_type=jnp.float32
        )
        product = product.reshape(9, chans_in, slab_len, rows_y, NZ)
        for index_y, offset_y in enumerate(OFFSETS):
            for index_z, offset_z in enumerate(OFFSETS):
                number = 3 * index_y + index_z
                running_grad = running_grad + jnp.roll(
                    product[number], (offset_y, offset_z), axis=(2, 3)
                )
    input_grad = running_grad.reshape(chans_in, slab_len, plane_size).astype(jnp.bfloat16)
    return (conv_out, input_grad)


def solution(mesh):
    in_specs = (
        P(("batch", "chan"), "slab", None),
        P(None, "chan", None),
        P(("batch", "chan"), "slab", None),
    )
    out_specs = (P(("batch", "chan"), "slab", None), P(("batch", "chan"), "slab", None))
    return jax.shard_map(
        per_device, mesh=mesh, in_specs=in_specs, out_specs=out_specs, check_vma=False
    )
```

profile of v0, /device:TPU:8, one launch (start us, length us, event | category | flops | bytes accessed | tf_op | source)
XLA Modules:
  0.0 322.6 jit_solution(15616600045513753703)
XLA Ops:
  7.9 1.0 fusion.86
  9.5 1.0 reshape.140
  10.6 1.1 fusion.31
  11.7 0.9 fusion.32
  14.4 1.1 fusion.57
  17.3 2.7 fusion.88
  27.8 1.4 copy-done.1
  29.2 2.8 add_bitcast_fusion
  32.1 5.4 %copy.11 = f32[512,2048]{1,0:T(8,128)} copy(f32[512,2048]{0,1:T(8,128)} %add_bitcast_fusion) | data formatting | bytes 8388608
  37.5 53.9 %all-gather.2.cloned.1.call-done = bf16[512,4,512]{2,1,0:T(4,128)(2,1)} async-done(((bf16[16,4,512]{2,1,0:T(4,128)(2,1)}), bf16[512,4,512]{2,1,0:T(4,128)(2,1)}) %all-gather.2.cloned.1.call-update) | async-done | bytes 2097168 | tf_op jit(solution)/shard_map/all_gather | solution.py:41
  91.4 2.2 copy.14
  96.0 1.5 fusion.69
  97.5 1.0 copy.6
  100.0 1.0 squeeze.98
  104.2 1.0 squeeze.91
  114.1 1.9 copy.7
  115.9 1.9 copy.9
  117.8 5.6 %pad_maximum_fusion.1 = (bf16[512,4,512]{2,1,0:T(4,128)(2,1)S(1)}, bf16[512,4,512]{2,1,0:T(4,128)(2,1)}) fusion(bf16[512,1,512]{2,1,0:T(2,128)(2,1)S(1)} %copy.7, bf16[512,4,512]{2,1,0:T(4,128)(2,1)S(1)} %copy-done, bf16[512,1,512]{2,1,0:T(2,128)(2,1)S(1)} %copy.9), kind=kLoop, calls=%fused_computation.4 | loop fusion | flops 8388608 | bytes 7340032 | tf_op jit(solution)/shard_map/concatenate | solution.py:20
  124.5 1.0 fusion.70
  139.6 1.0 squeeze.103
  140.6 1.0 squeeze.85
  141.7 1.0 add_convert_fusion
  142.7 171.0 %reduce-scatter.4.cloned.1.call-done = f32[16,2048]{1,0:T(8,128)} async-done(((f32[512,2048]{1,0:T(8,128)}), f32[16,2048]{1,0:T(8,128)}) %reduce-scatter.4.cloned.1.call-update) | async-done | bytes 131088
  313.7 1.2 copy.12
  (259 shorter events, 43.9 us)
Async XLA Ops:
  7.2 84.2 %all-gather.2.cloned.1.call-start = ((), (), s32[]{:S(2)}) async-start(), calls=%async_computation.1 | async-start | bytes 2162688 | tf_op jit(solution)/shard_map/all_gather | solution.py:41
  7.9 305.9 %reduce-scatter.4.cloned.1.call-start = ((), (), s32[]{:S(2)}) async-start(), calls=%async_computation.2 | async-start | bytes 4325376
  8.9 11.1 %collective-permute-start = (bf16[16,1,512]{2,1,0:T(2,128)(2,1)S(1)}, bf16[16,1,512]{2,1,0:T(2,128)(2,1)S(1)}, u32[]{:S(2)}, u32[]{:S(2)}) collective-permute-start(bf16[16,1,512]{2,1,0:T(2,128)(2,1)S(1)} %get-tuple-element.91), channel_id=1, source_target_pairs={{0,4},{4,0},{1,5},{5,1},{2,6},{6,2},{3,7},{7,3},{8,12},{12,8},{9,1... | collective-permute-start | bytes 49160 | tf_op jit(solution)/shard_map/ppermute | solution.py:16
  9.0 11.0 %collective-permute-start.1 = (bf16[16,1,512]{2,1,0:T(2,128)(2,1)S(1)}, bf16[16,1,512]{2,1,0:T(2,128)(2,1)S(1)}, u32[]{:S(2)}, u32[]{:S(2)}) collective-permute-start(bf16[16,1,512]{2,1,0:T(2,128)(2,1)S(1)} %get-tuple-element.90), channel_id=1, source_target_pairs={{4,0},{0,4},{5,1},{1,5},{6,2},{2,6},{7,3},{3,7},{12,8},{8,12},{13,... | collective-permute-start | bytes 49160 | tf_op jit(solution)/shard_map/ppermute | solution.py:19
  10.6 2.9 copy-start.7
  11.7 2.6 copy-start.33
  13.5 2.2 copy-start.31
  27.0 2.2 copy-start.1
  98.4 15.6 %collective-permute-start.2 = (bf16[512,1,512]{2,0,1:T(8,128)(2,1)}, bf16[512,1,512]{2,0,1:T(8,128)(2,1)}, u32[]{:S(2)}, u32[]{:S(2)}) collective-permute-start(bf16[512,1,512]{2,0,1:T(8,128)(2,1)} %copy.6), channel_id=1, source_target_pairs={{4,0},{0,4},{5,1},{1,5},{6,2},{2,6},{7,3},{3,7},{12,8},{8,12},{13,... | collective-permute-start | bytes 1572872 | tf_op jit(solution)/shard_map/ppermute | solution.py:19
  99.4 16.6 %collective-permute-start.3 = (bf16[512,1,512]{2,0,1:T(8,128)(2,1)}, bf16[512,1,512]{2,0,1:T(8,128)(2,1)}, u32[]{:S(2)}, u32[]{:S(2)}) collective-permute-start(bf16[512,1,512]{2,0,1:T(8,128)(2,1)} %copy.8), channel_id=1, source_target_pairs={{0,4},{4,0},{1,5},{5,1},{2,6},{6,2},{3,7},{7,3},{8,12},{12,8},{9,1... | collective-permute-start | bytes 1572872 | tf_op jit(solution)/shard_map/ppermute | solution.py:16
  103.0 2.9 copy-start.5
  105.9 2.4 copy-start.6
  106.7 2.4 copy-start.8
  107.5 2.4 copy-start.25
  110.4 2.0 copy-start.21
  139.0 2.6 copy-start.9
  139.0 2.6 copy-start.10
  139.1 2.6 copy-start.11
  139.1 2.6 copy-start.12
  139.1 2.6 copy-start.13
  139.1 2.6 copy-start.14
  139.1 2.6 copy-start.15
  139.1 2.6 copy-start.16
  139.1 2.6 copy-start.29
  (21 other events, 23.8 us)
Sparse Core Ops, SparseCore 0:
  10.6 80.7 all-gather.1
  95.3 218.4 reduce-scatter.3
where the time goes:
time: 323 us
  waiting for transfers between devices  226 us (70%)
  local copies, waits for them, and re-layouts  50.9 us (16%)
  other arithmetic  22 us (7%)
  between operations  15.1 us (5%)
  matrix products  7.79 us (2%)
    unnamed x3, waiting for transfers between devices  172 us
    all_gather x1, waiting for transfers between devices, per_device(): grad_all = lax.all_gather(out_grad, 'chan', axis=0, tiled=True)  53.9 us
    unnamed x83, local copies, waits for them, and re-layouts  14.6 us
    concatenate x20, local copies, waits for them, and re-layouts, per_device(): jnp.roll(product[number], (offset_y, offset_z), axis=(2, 3))  7.88 us
    squeeze x27, local copies, waits for them, and re-layouts, per_device(): product[number]  7 us
    concatenate x32, other arithmetic, per_device(): jnp.roll(product[number], (offset_y, offset_z), axis=(2, 3))  6.98 us
  transfers between devices with their start and end apart: 6, of which 2 were waited for; matrix products, arithmetic and copies ran while one was open for 23% of the time, Pallas kernels for 0%

commit v1 on v0

--- a/solution.py
+++ b/solution.py
@@ -38,7 +38,9 @@
     rows_y = plane_size // NZ
     cell_count = slab_len * plane_size
     halo_in = padded(inputs, (("slab", 1),), 1)
-    grad_all = lax.all_gather(out_grad, "chan", axis=0, tiled=True)
+    grad_all = jnp.concatenate(
+        lax.all_to_all(jnp.stack([out_grad] * lax.axis_size("chan")), "chan", 0, 0), axis=0
+    )
     halo_grad = padded(grad_all, (("slab", 1),), 1)
     columns = [
         stack_yz(halo_in[:, 1 + offset_x : 1 + offset_x + slab_len], rows_y) for offset_x in OFFSETS

time: 323 us -> 315 us (0.975)
  waiting for transfers between devices: 226 us -> 176 us
  other arithmetic: 22 us -> 40.7 us
  starting transfers between devices: 1.17 us -> 12.6 us
  local copies, waits for them, and re-layouts: 50.9 us -> 61.6 us
    all_gather x1 -> x0, waiting for transfers between devices: 53.9 us -> none  [per_device(): grad_all = lax.all_gather(out_grad, 'chan', axis=0, tiled=True)]
    unnamed x21, other arithmetic: 3.61 us -> 21.7 us
    all_to_all x0 -> x1, starting transfers between devices: none -> 11.4 us  [per_device(): lax.all_to_all(jnp.stack([out_grad] * lax.axis_size('chan')), 'chan', 0, 0)]
    slice x1 -> x2, local copies, waits for them, and re-layouts: 0.94 us -> 5.68 us  [per_device(): halo_grad[:, 1 - offset_x:1 - offset_x + slab_len]]
    unnamed x3 -> x2, waiting for transfers between devices: 172 us -> 176 us
    reshape x3, local copies, waits for them, and re-layouts: 2.67 us -> 6.48 us  [stack_yz(): return jnp.stack(pieces).reshape(9 * chans, slab_len * plane_size)]
    ppermute x2 -> x0, local copies, waits for them, and re-layouts: 3.71 us -> none  [the longest x1 1.85 us: padded(): lax.ppermute(lax.slice_in_dim(block, block.shape[dim] - width, None, axis...]
    unnamed x83 -> x98, local copies, waits for them, and re-layouts: 14.6 us -> 16.8 us
  transfers between devices with their start and end apart: 6 -> 6, of which waited for: 2 -> 1; matrix products, arithmetic and copies ran while one was open for 23% -> 32% of each run, Pallas kernels for 0% -> 0%
where the time goes in v1:
time: 315 us; the launch traced here: 314 us
  waiting for transfers between devices  176 us (56%)
  local copies, waits for them, and re-layouts  61.6 us (20%)
  other arithmetic  40.7 us (13%)
  between operations  15.1 us (5%)
  starting transfers between devices  12.6 us (4%)
  matrix products  8.45 us (3%)
    unnamed x2, waiting for transfers between devices  176 us
    unnamed x21, other arithmetic  21.7 us
    unnamed x98, local copies, waits for them, and re-layouts  16.8 us
    all_to_all x1, starting transfers between devices, per_device(): lax.all_to_all(jnp.stack([out_grad] * lax.axis_size('chan')), 'chan', 0, 0)  11.4 us
    concatenate x20, local copies, waits for them, and re-layouts, per_device(): jnp.roll(product[number], (offset_y, offset_z), axis=(2, 3))  7.84 us
    reshape x3, local copies, waits for them, and re-layouts, stack_yz(): return jnp.stack(pieces).reshape(9 * chans, slab_len * plane_size)  6.48 us
    dot_general x3, matrix products, per_device(): lax.dot_general(partial_weight_x, columns[partial_index_x], (((0,), (0,))...  6.33 us
  transfers between devices with their start and end apart: 6, of which 1 were waited for; matrix products, arithmetic and copies ran while one was open for 32% of the time, Pallas kernels for 0%

profile of v1, /device:TPU:8, one launch (start us, length us, event | category | flops | bytes accessed | tf_op | source)
XLA Modules:
  0.0 314.3 jit_solution(1632847715982125128)
XLA Ops:
  8.0 1.6 stack.155
  9.6 11.4 %all-to-all-start = ((bf16[32,16,4,512]{3,1,2,0:T(8,128)(2,1)}), bf16[32,16,4,512]{3,1,2,0:T(8,128)(2,1)S(1)}, u32[]{:S(2)}, u32[]{:S(2)}) async-start(bf16[32,16,4,512]{3,1,2,0:T(8,128)(2,1)} %stack.155), calls=%async_computation | async-start | bytes 4194304 | tf_op jit(solution)/shard_map/all_to_all | solution.py:42
  26.5 1.8 fusion.73
  28.4 1.8 fusion.57
  30.9 1.7 fusion.58
  37.1 2.2 reshape.143
  39.2 2.7 fusion.88
  48.6 1.8 fusion.63
  51.2 1.7 fusion.64
  52.9 1.7 fusion.65
  54.6 1.6 constant_dynamic-update-slice_fusion.2
  56.2 1.7 fusion.66
  60.1 2.2 reshape.146
  70.2 2.2 reshape.140
  73.1 1.4 copy-done
  74.5 2.8 add_bitcast_fusion
  77.3 5.5 %copy.25 = f32[512,2048]{1,0:T(8,128)} copy(f32[512,2048]{0,1:T(8,128)} %add_bitcast_fusion) | data formatting | bytes 8388608
  82.9 2.0 copy.22
  88.2 1.4 copy-done.1
  101.7 3.6 %pad_maximum_fusion.1 = (bf16[512,4,512]{2,0,1:T(8,128)(2,1)}, bf16[512,4,512]{2,0,1:T(8,128)(2,1)}) fusion(bf16[512,1,512]{2,0,1:T(8,128)(2,1)} %collective-permute-done.2, bf16[512,4,512]{2,0,1:T(8,128)(2,1)S(1)} %bitcast.191, bf16[512,1,512]{2,0,1:T(8,128)(2,1)} %collective-permute-done.3), kind=kLoop, calls=%fused_computation.4 | loop fusion | flops 2097152 | bytes 7340032 | tf_op jit(solution)/shard_map/concatenate | solution.py:20
  105.3 2.8 copy.21
  111.5 2.9 copy.23
  129.6 175.8 %reduce-scatter.4.cloned.1.call-done = f32[16,2048]{1,0:T(8,128)} async-done(((f32[512,2048]{1,0:T(8,128)}), f32[16,2048]{1,0:T(8,128)}) %reduce-scatter.4.cloned.1.call-update) | async-done | bytes 131088
  305.4 1.2 copy.26
  (274 shorter events, 63.8 us)
Async XLA Ops:
  9.6 11.5 %copy-start.9 = (bf16[16,4,512]{2,1,0:T(4,128)(2,1)S(1)}, bf16[16,4,512]{2,1,0:T(4,128)(2,1)}, u32[]{:S(2)}) copy-start(bf16[16,4,512]{2,1,0:T(4,128)(2,1)} %param.3) | copy-start | bytes 196612
  9.6 73.2 %all-to-all-start = ((bf16[32,16,4,512]{3,1,2,0:T(8,128)(2,1)}), bf16[32,16,4,512]{3,1,2,0:T(8,128)(2,1)S(1)}, u32[]{:S(2)}, u32[]{:S(2)}) async-start(bf16[32,16,4,512]{3,1,2,0:T(8,128)(2,1)} %stack.155), calls=%async_computation | async-start | bytes 4194304 | tf_op jit(solution)/shard_map/all_to_all | solution.py:42
  21.1 284.3 %reduce-scatter.4.cloned.1.call-start = ((), (), s32[]{:S(2)}) async-start(), calls=%async_computation.2 | async-start | bytes 4325376
  21.2 20.8 %collective-permute-start = (bf16[16,1,512]{2,1,0:T(2,128)(2,1)S(1)}, bf16[16,1,512]{2,1,0:T(2,128)(2,1)S(1)}, u32[]{:S(2)}, u32[]{:S(2)}) collective-permute-start(bf16[16,1,512]{2,1,0:T(2,128)(2,1)S(1)} %get-tuple-element.97), channel_id=1, source_target_pairs={{0,4},{4,0},{1,5},{5,1},{2,6},{6,2},{3,7},{7,3},{8,12},{12,8},{9,1... | collective-permute-start | bytes 49160 | tf_op jit(solution)/shard_map/ppermute | solution.py:16
  21.3 20.7 %collective-permute-start.1 = (bf16[16,1,512]{2,1,0:T(2,128)(2,1)S(1)}, bf16[16,1,512]{2,1,0:T(2,128)(2,1)}, u32[]{:S(2)}, u32[]{:S(2)}) collective-permute-start(bf16[16,1,512]{2,1,0:T(2,128)(2,1)S(1)} %get-tuple-element.96), channel_id=1, source_target_pairs={{4,0},{0,4},{5,1},{1,5},{6,2},{2,6},{7,3},{3,7},{12,8},{8,12},{13,... | collective-permute-start | bytes 49160 | tf_op jit(solution)/shard_map/ppermute | solution.py:19
  26.5 6.1 %copy-start.37 = (bf16[16,4,8,63]{3,2,1,0:T(8,128)(2,1)S(1)}, bf16[16,4,8,63]{3,2,1,0:T(8,128)(2,1)}, u32[]{:S(2)}) copy-start(bf16[16,4,8,63]{3,2,1,0:T(8,128)(2,1)} %get-tuple-element.83) | copy-start | bytes 193540
  26.5 6.1 %copy-start.38 = (bf16[16,4,8,1]{3,2,1,0:T(8,128)(2,1)S(1)}, bf16[16,4,8,1]{3,2,1,0:T(8,128)(2,1)}, u32[]{:S(2)}) copy-start(bf16[16,4,8,1]{3,2,1,0:T(8,128)(2,1)} %get-tuple-element.85) | copy-start | bytes 3076
  26.5 6.9 %copy-start.39 = (bf16[1,16,4,8,64]{4,3,2,1,0:T(8,128)(2,1)S(1)}, bf16[1,16,4,8,64]{4,3,2,1,0:T(8,128)(2,1)}, u32[]{:S(2)}) copy-start(bf16[1,16,4,8,64]{4,3,2,1,0:T(8,128)(2,1)} %stack.139) | copy-start | bytes 196612
  26.5 7.5 %copy-start.34 = (bf16[16,4,8,63]{3,2,1,0:T(8,128)(2,1)S(1)}, bf16[16,4,8,63]{3,2,1,0:T(8,128)(2,1)}, u32[]{:S(2)}) copy-start(bf16[16,4,8,63]{3,2,1,0:T(8,128)(2,1)} %get-tuple-element.82) | copy-start | bytes 193540
  26.5 7.5 %copy-start.35 = (bf16[16,4,8,1]{3,2,1,0:T(8,128)(2,1)S(1)}, bf16[16,4,8,1]{3,2,1,0:T(8,128)(2,1)}, u32[]{:S(2)}) copy-start(bf16[16,4,8,1]{3,2,1,0:T(8,128)(2,1)} %get-tuple-element.84) | copy-start | bytes 3076
  28.4 10.9 %copy-start.3 = (bf16[9,16,512]{2,1,0:T(8,128)(2,1)}, bf16[9,16,512]{2,1,0:T(8,128)(2,1)S(1)}, u32[]{:S(2)}) copy-start(bf16[9,16,512]{2,1,0:T(8,128)(2,1)S(1)} %get-tuple-element.45) | copy-start | bytes 442372
  48.6 4.3 %copy-start.36 = (bf16[16,4,8,1]{3,2,1,0:T(8,128)(2,1)S(1)}, bf16[16,4,8,1]{3,2,1,0:T(8,128)(2,1)}, u32[]{:S(2)}) copy-start(bf16[16,4,8,1]{3,2,1,0:T(8,128)(2,1)} %get-tuple-element.77) | copy-start | bytes 3076
  48.6 9.3 %copy-start.32 = (bf16[16,4,8,63]{3,2,1,0:T(8,128)(2,1)S(1)}, bf16[16,4,8,63]{3,2,1,0:T(8,128)(2,1)}, u32[]{:S(2)}) copy-start(bf16[16,4,8,63]{3,2,1,0:T(8,128)(2,1)} %get-tuple-element.47) | copy-start | bytes 193540
  48.6 9.3 %copy-start.33 = (bf16[16,4,8,1]{3,2,1,0:T(8,128)(2,1)S(1)}, bf16[16,4,8,1]{3,2,1,0:T(8,128)(2,1)}, u32[]{:S(2)}) copy-start(bf16[16,4,8,1]{3,2,1,0:T(8,128)(2,1)} %get-tuple-element.49) | copy-start | bytes 3076
  59.4 2.9 copy-start.40
  90.7 11.0 %collective-permute-start.2 = (bf16[512,1,512]{2,0,1:T(8,128)(2,1)}, bf16[512,1,512]{2,0,1:T(8,128)(2,1)}, u32[]{:S(2)}, u32[]{:S(2)}) collective-permute-start(bf16[512,1,512]{2,0,1:T(8,128)(2,1)} %get-tuple-element.14), channel_id=1, source_target_pairs={{4,0},{0,4},{5,1},{1,5},{6,2},{2,6},{7,3},{3,7},{12,8},{8,12},{13,... | collective-permute-start | bytes 1572872 | tf_op jit(solution)/shard_map/ppermute | solution.py:19
  90.8 10.9 %collective-permute-start.3 = (bf16[512,1,512]{2,0,1:T(8,128)(2,1)}, bf16[512,1,512]{2,0,1:T(8,128)(2,1)}, u32[]{:S(2)}, u32[]{:S(2)}) collective-permute-start(bf16[512,1,512]{2,0,1:T(8,128)(2,1)} %get-tuple-element.15), channel_id=1, source_target_pairs={{0,4},{4,0},{1,5},{5,1},{2,6},{6,2},{3,7},{7,3},{8,12},{12,8},{9,1... | collective-permute-start | bytes 1572872 | tf_op jit(solution)/shard_map/ppermute | solution.py:16
  93.6 4.0 %copy-start.26 = (f32[16,2048]{1,0:T(8,128)S(1)}, f32[16,2048]{1,0:T(8,128)}, u32[]{:S(2)}) copy-start(f32[16,2048]{1,0:T(8,128)} %get-tuple-element.31) | copy-start | bytes 393220
  99.0 2.7 copy-start.2
  111.5 3.0 copy-start.7
  111.5 2.9 copy-start.6
  126.0 2.6 copy-start.10
  126.0 2.6 copy-start.11
  126.0 2.6 copy-start.12
  (29 other events, 42.9 us)
Sparse Core Ops, SparseCore 0:
  83.0 222.3 reduce-scatter.3
